TPU v7x, 256 devices: a whole 4x4x8 slice. The times are simulated.
256 devices in a mesh: cond: 2 (over x_hi), gx: 8 (over z), gy: 16 (over x_lo, y, core).
Axes of the slice: x: 4 (x_hi: 2, x_lo: 2; x = x_hi * 2 + x_lo), y: 4, z: 8, core: 2. Of those that a mesh axis runs over, the one named last changes fastest.
Arguments:
- psi_old: float32 [64, 4, 6, 8192], P('gx', 'cond', None, 'gy'), may hold values from -6 to 6
- objective_grad: float32 [64, 4, 6, 8192], P('gx', 'cond', None, 'gy'), may hold values from -6 to 6
- near_upper: float32 [64, 4, 6, 6, 8192], P('gx', 'cond', None, None, 'gy'), may hold values from -1 to 0.06
- far_upper: float32 [64, 4, 6, 6, 8192], P('gx', 'cond', None, None, 'gy'), may hold values from -1 to 0.03
- inverse_diag: float32 [64, 4, 6, 6, 8192], P('gx', 'cond', None, None, 'gy'), may hold values from -0.06 to 1
- near_lower: float32 [64, 4, 6, 6, 8192], P('gx', 'cond', None, None, 'gy'), may hold values from -1 to 0.06
- far_lower: float32 [64, 4, 6, 6, 8192], P('gx', 'cond', None, None, 'gy'), may hold values from -1 to 0.03
- y_inverse: float32 [64, 4, 6, 6, 8192], P('gx', 'cond', None, None, 'gy'), may hold values from -0.1 to 1.5
- z_inverse: float32 [4, 6, 32, 32], P('cond'), may hold values from -1 to 1
- sens_terms: float32 [64, 4, 3, 6, 8192], P('gx', 'cond', None, None, 'gy'), may hold values from -1.25 to 1.25
- wall_mask: int32 [64, 8192], P('gx', 'gy'), may hold values 0 or 1
- cond_index: int32 [4], P('cond'), may hold values from 0 to 7
- weight_table: float32 [8], replicated, may hold values from 0.5 to 2
Outputs:
- psi_new: float32 [64, 4, 6, 8192], P('gx', 'cond', None, 'gy')
- mesh_sens: float32 [64, 3, 8192], P('gx', None, 'gy')
All inputs are finite; a program needn't handle non-finite values. No bound on the sum of `wall_mask` on one device may be relied on, other than what follows from the above.
Results may differ from a plain program's by a relative error of at most 0.0001.
Values sent between devices are 32-bit elements; how exact they have to be, the bound alone decides.
A program may use at most 128 MiB of HBM per device.

v0:
```python
import jax
import jax.numpy as jnp
from jax import lax
from jax.sharding import PartitionSpec as P

NZ = 32
ITERS = 2


def extended(value, sides, width):
    for axis, dim in sides:
        size, length = (lax.axis_size(axis), value.shape[dim])
        up = [(i, (i + 1) % size) for i in range(size - 1)]
        down = [(j, i) for i, j in up]
        last = lax.slice_in_dim(value, length - width, length, axis=dim)
        first = lax.slice_in_dim(value, 0, width, axis=dim)
        before = lax.ppermute(last, axis, up)
        after = lax.ppermute(first, axis, down)
        value = jnp.concatenate([before, value, after], axis=dim)
    return value


def from_behind(value, axis, steps):
    count = lax.axis_size(axis)
    first, last = (max(0, -steps), min(count, count - steps))
    return lax.ppermute(value, axis, [(source, source + steps) for source in range(first, last)])


def apply_block(blocks, vector):
    return jnp.sum(blocks * vector[..., None, :, :], axis=-2)


def apply_transpose(blocks, vector):
    return jnp.sum(blocks * vector[..., :, None, :], axis=-3)


def upper_sweep(rhs, near, far, incoming):

    def step(carry, item):
        last, before = carry
        value, near_cell, far_cell = item
        now = value - apply_block(near_cell, last) - apply_block(far_cell, before)
        return ((now, last), now)

    carry, values = lax.scan(step, (incoming[0], incoming[1]), (rhs, near, far))
    return (values, jnp.stack([carry[0], carry[1]]))


def lower_sweep(rhs, inverse, near, far, incoming):

    def step(carry, item):
        pending, partial_value = carry
        value, inverse_cell, near_cell, far_cell = item
        now = apply_transpose(inverse_cell, value - pending)
        return (
            (partial_value + apply_transpose(near_cell, now), apply_transpose(far_cell, now)),
            now,
        )

    carry, values = lax.scan(
        step, (incoming[0], incoming[1]), (rhs, inverse, near, far), reverse=True
    )
    return (values, jnp.stack([carry[0], carry[1]]))


def unit_carries(shape):
    width = 2 * shape[1]
    table = jnp.eye(width, dtype=jnp.float32).reshape(width, 2, shape[1]).transpose(1, 0, 2)
    return jnp.broadcast_to(table[:, :, None, :, None], (2, width, shape[0], shape[1], shape[2]))


def as_matrix(response):
    width = response.shape[1]
    return jnp.transpose(response, (1, 0, 3, 2, 4)).reshape(
        width, width, response.shape[2], response.shape[4]
    )


def as_vector(carry):
    return jnp.transpose(carry, (0, 2, 1, 3)).reshape(-1, carry.shape[1], carry.shape[3])


def from_vector(vector, count):
    return vector.reshape(2, count, vector.shape[1], vector.shape[2]).transpose(0, 2, 1, 3)


def carry_through(vector, matrix, offset):
    return jnp.einsum("kcl,kmcl->mcl", vector, matrix, precision=lax.Precision.HIGHEST) + offset


def on_device(
    psi_old,
    objective_grad,
    near_upper,
    far_upper,
    inverse_diag,
    near_lower,
    far_lower,
    y_inverse,
    z_inverse,
    sens_terms,
    wall_mask,
    cond_index,
    weight_table,
):
    keep = (1.0 - wall_mask.astype(jnp.float32))[:, None, None, :]
    carry_shape = psi_old.shape[1:]
    zeros = jnp.zeros((2,) + carry_shape, jnp.float32)
    psi = psi_old
    for step in range(ITERS):
        stream_pad = extended(psi, (("gx", 0),), 1)
        span_pad = extended(psi, (("gy", 3),), NZ)
        beside_all = (
            stream_pad[2:] + stream_pad[:-2] + span_pad[..., 2 * NZ :] + span_pad[..., : -2 * NZ]
        )
        rhs = objective_grad + 0.5 * beside_all - 2.0 * psi
        grid = rhs.reshape(rhs.shape[0], rhs.shape[1], rhs.shape[2], rhs.shape[3] // NZ, NZ)
        zres = jnp.einsum(
            "icvjq,cvqk->icvjk", grid, z_inverse, precision=lax.Precision.HIGHEST
        ).reshape(rhs.shape)
        yres = apply_transpose(y_inverse, zres)
        blank = jnp.zeros((yres.shape[0], 1) + carry_shape, jnp.float32)
        units = unit_carries(carry_shape)
        values, offset = upper_sweep(yres, near_upper, far_upper, zeros)
        values, response = upper_sweep(blank, near_upper, far_upper, units)
        matrix = as_matrix(response)
        vector = as_vector(offset)

        def upper_reversal(turn, incoming):
            return from_behind(carry_through(incoming, matrix, vector), "gx", 1)

        entering = lax.fori_loop(0, lax.axis_size("gx") - 1, upper_reversal, jnp.zeros_like(vector))
        upper, leaving = upper_sweep(
            yres, near_upper, far_upper, from_vector(entering, carry_shape[1])
        )
        values, offset = lower_sweep(upper, inverse_diag, near_lower, far_lower, zeros)
        values, response = lower_sweep(blank, inverse_diag, near_lower, far_lower, units)
        reverse_matrix = as_matrix(response)
        vector_back = as_vector(offset)

        def lower_turn(turn, incoming):
            return from_behind(carry_through(incoming, reverse_matrix, vector_back), "gx", -1)

        entering = lax.fori_loop(
            0, lax.axis_size("gx") - 1, lower_turn, jnp.zeros_like(vector_back)
        )
        lower, leaving = lower_sweep(
            upper, inverse_diag, near_lower, far_lower, from_vector(entering, carry_shape[1])
        )
        psi = (psi + 0.05 * lower) * keep
    onehot = (cond_index[:, None] == jnp.arange(weight_table.shape[0])[None, :]).astype(jnp.float32)
    weights = jnp.sum(onehot * weight_table[None, :], axis=1)
    local_sens = jnp.einsum(
        "icvl,icmvl->iml",
        psi * weights[None, :, None, None],
        sens_terms,
        precision=lax.Precision.HIGHEST,
    )
    mesh_sens = lax.psum(local_sens, "cond")
    return (psi, mesh_sens)


def solution(mesh):
    placed = (
        P("gx", "cond", None, "gy"),
        P("gx", "cond", None, "gy"),
        P("gx", "cond", None, None, "gy"),
        P("gx", "cond", None, None, "gy"),
        P("gx", "cond", None, None, "gy"),
        P("gx", "cond", None, None, "gy"),
        P("gx", "cond", None, None, "gy"),
        P("gx", "cond", None, None, "gy"),
        P("cond", None, None, None),
        P("gx", "cond", None, None, "gy"),
        P("gx", "gy"),
        P("cond"),
        P(),
    )
    return jax.shard_map(
        on_device,
        mesh=mesh,
        in_specs=placed,
        out_specs=(P("gx", "cond", None, "gy"), P("gx", None, "gy")),
        check_vma=False,
    )
```

profile of v0, /device:TPU:8, one launch (start us, length us, event | category | flops | bytes accessed | tf_op | source)
XLA Modules:
  0.0 447.8 jit_solution(16862666755079714882)
XLA Ops:
  14.9 34.7 %while.203 = (s32[]{:T(128)}, f32[12,2,6,512]{3,1,2,0:T(2,128)S(1)}, f32[12,2,6,512]{3,1,2,0:T(2,128)S(1)}, f32[8,2,6,6,512]{4,1,3,2,0:T(2,128)}, f32[8,2,6,6,512]{4,1,3,2,0:T(2,128)}, /*index=5*/s32[]{:T(128)}) while((s32[]{:T(128)}, f32[12,2,6,512]{3,1,2,0:T(2,128)S(1)}, f32[12,2,6,512]{3,1,2,0:T(2,128)S(1)}, ...), condition=%wide.region_8.9_spmd, body=%wide.region_5.8_spmd.sunk | while | flops 1769474 | bytes 3539021 | solution.py:45
  49.9 38.1 %while.202 = (s32[]{:T(128)}, f32[12,2,6,512]{3,1,2,0:T(2,128)S(1)}, f32[12,2,6,512]{3,1,2,0:T(2,128)S(1)}, f32[8,2,6,6,512]{4,1,3,2,0:T(2,128)}, f32[8,2,6,6,51...) while((s32[]{:T(128)}, f32[12,2,6,512]{3,1,2,0:T(2,128)S(1)}, ...), condition=%wide.region_4.5_spmd, body=%wide.region_0.4_spmd.sunk | while | flops 2580483 | bytes 4866153 | solution.py:60
  96.1 9.2 %while.212 = (s32[]{:T(128)}, f32[2,6,512]{2,0,1:T(2,128)S(1)}, f32[2,6,512]{2,0,1:T(2,128)S(1)}, f32[8,2,6,512]{3,1,2,0:T(2,128)S(1)}, f32[8,2,6,6,512]{4,1,3,2...) while((s32[]{:T(128)}, f32[2,6,512]{2,0,1:T(2,128)S(1)}, ...), condition=%wide.region_13.14_spmd.clone, body=%wide.region_10.13_spmd.clone.sunk | while | flops 153603 | bytes 589927 | solution.py:45
  105.4 46.8 %while.204 = (s32[]{:T(128)}, f32[12,2,512]{2,1,0:T(2,128)S(1)}, f32[12,12,2,512]{3,2,1,0:T(2,128)S(1)}, f32[12,2,512]{2,1,0:T(2,128)S(1)}, s32[]{:T(128)}) while((s32[]{:T(128)}, f32[12,2,512]{2,1,0:T(2,128)S(1)}, f32[12,12,2,512]{3,2,1,0:T(2,128)S(1)}, f32[12,2,512]{2,1,0:T(2,128)S(1)}, s32[]{:T(128)}) %tuple.404), condition=%wide.region_15.16_spmd, body=%wide.region_14.15_spmd.sunk | while | flops 294914 | bytes 1032293 | solution.py:132
  152.2 9.3 %while.205 = (s32[]{:T(128)}, f32[2,6,512]{2,0,1:T(2,128)S(1)}, f32[2,6,512]{2,0,1:T(2,128)S(1)}, f32[8,2,6,512]{3,1,2,0:T(2,128)S(1)}, f32[8,2,6,512]{3,1,2,0:T...) while((s32[]{:T(128)}, f32[2,6,512]{2,0,1:T(2,128)S(1)}, ...), condition=%wide.region_19.20_spmd, body=%wide.region_16.19_spmd.sunk | while | flops 159746 | bytes 639073 | solution.py:45
  161.6 17.8 %while.213 = (s32[]{:T(128)}, f32[2,6,512]{2,0,1:T(2,128)S(1)}, f32[2,6,512]{2,0,1:T(2,128)S(1)}, f32[8,2,6,6,512]{4,1,3,2,0:T(2,128)}, f32[8,2,6,6,512]{4,1,3,2...) while((s32[]{:T(128)}, f32[2,6,512]{2,0,1:T(2,128)S(1)}, ...), condition=%wide.region_24.25_spmd.clone, body=%wide.region_20.24_spmd.clone.sunk | while | flops 221188 | bytes 761991 | solution.py:60
  179.5 53.7 %while.206 = (s32[]{:T(128)}, f32[12,2,512]{2,1,0:T(2,128)S(1)}, f32[12,12,2,512]{3,2,1,0:T(2,128)S(1)}, f32[12,2,512]{2,1,0:T(2,128)S(1)}, s32[]{:T(128)}) while((s32[]{:T(128)}, f32[12,2,512]{2,1,0:T(2,128)S(1)}, f32[12,12,2,512]{3,2,1,0:T(2,128)S(1)}, f32[12,2,512]{2,1,0:T(2,128)S(1)}, s32[]{:T(128)}) %tuple.405), condition=%wide.region_26.27_spmd, body=%wide.region_25.26_spmd.sunk | while | flops 294914 | bytes 1032293 | solution.py:144
  181.1 6.5 %collective-permute-done.1 = f32[12,2,512]{2,1,0:T(2,128)S(1)} collective-permute-done((f32[12,2,512]{2,1,0:T(2,128)S(1)}, f32[12,2,512]{2,1,0:T(2,128)S(1)}, u32[]{:S(2)}, u32[]{:S(2)}) %collective-permute-start.1) | collective-permute-done | bytes 49184 | tf_op jit(solution)/shard_map/while/body/eval_jaxpr/ppermute | solution.py:26
  196.7 6.2 %collective-permute-done.1 = f32[12,2,512]{2,1,0:T(2,128)S(1)} collective-permute-done((f32[12,2,512]{2,1,0:T(2,128)S(1)}, f32[12,2,512]{2,1,0:T(2,128)S(1)}, u32[]{:S(2)}, u32[]{:S(2)}) %collective-permute-start.1) | collective-permute-done | bytes 49184 | tf_op jit(solution)/shard_map/while/body/eval_jaxpr/ppermute | solution.py:26
  204.5 6.2 %collective-permute-done.1 = f32[12,2,512]{2,1,0:T(2,128)S(1)} collective-permute-done((f32[12,2,512]{2,1,0:T(2,128)S(1)}, f32[12,2,512]{2,1,0:T(2,128)S(1)}, u32[]{:S(2)}, u32[]{:S(2)}) %collective-permute-start.1) | collective-permute-done | bytes 49184 | tf_op jit(solution)/shard_map/while/body/eval_jaxpr/ppermute | solution.py:26
  233.3 18.1 %while.207 = (s32[]{:T(128)}, f32[2,6,512]{2,0,1:T(2,128)S(1)}, f32[2,6,512]{2,0,1:T(2,128)S(1)}, f32[8,2,6,512]{3,1,2,0:T(2,128)S(1)}, f32[8,2,6,6,512]{4,1,3,2...) while((s32[]{:T(128)}, f32[2,6,512]{2,0,1:T(2,128)S(1)}, ...), condition=%wide.region_31.32_spmd, body=%wide.region_27.31_spmd.sunk | while | flops 215043 | bytes 811137 | solution.py:60
  257.4 6.0 %collective-permute-start.9 = (f32[1,2,6,512]{3,1,2,0:T(2,128)S(1)}, f32[1,2,6,512]{3,1,2,0:T(2,128)S(1)}, u32[]{:S(2)}, u32[]{:S(2)}) collective-permute-start(f32[1,2,6,512]{3,1,2,0:T(2,128)S(1)} %get-tuple-element.1338), channel_id=1, source_target_pairs={{0,16},{16,32},{32,48},{48,64},{64,80},{80,96},{96,112},{1,17},{17... | collective-permute-start | bytes 73736 | tf_op jit(solution)/shard_map/ppermute | solution.py:17
  273.5 9.2 %while.214 = (s32[]{:T(128)}, f32[2,6,512]{2,0,1:T(2,128)S(1)}, f32[2,6,512]{2,0,1:T(2,128)S(1)}, f32[8,2,6,512]{3,1,2,0:T(2,128)S(1)}, f32[8,2,6,6,512]{4,1,3,2...) while((s32[]{:T(128)}, f32[2,6,512]{2,0,1:T(2,128)S(1)}, ...), condition=%wide.region_36.37_spmd.clone, body=%wide.region_33.36_spmd.clone.sunk | while | flops 153603 | bytes 589927 | solution.py:45
  282.8 51.7 %while.208 = (s32[]{:T(128)}, f32[12,2,512]{2,1,0:T(2,128)S(1)}, f32[12,12,2,512]{3,2,1,0:T(2,128)S(1)}, f32[12,2,512]{2,1,0:T(2,128)S(1)}, s32[]{:T(128)}) while((s32[]{:T(128)}, f32[12,2,512]{2,1,0:T(2,128)S(1)}, f32[12,12,2,512]{3,2,1,0:T(2,128)S(1)}, f32[12,2,512]{2,1,0:T(2,128)S(1)}, s32[]{:T(128)}) %tuple.402), condition=%wide.region_38.39_spmd, body=%wide.region_37.38_spmd.sunk | while | flops 294914 | bytes 1032293 | solution.py:132
  334.6 9.3 %while.209 = (s32[]{:T(128)}, f32[2,6,512]{2,0,1:T(2,128)S(1)}, f32[2,6,512]{2,0,1:T(2,128)S(1)}, f32[8,2,6,512]{3,1,2,0:T(2,128)S(1)}, f32[8,2,6,512]{3,1,2,0:T...) while((s32[]{:T(128)}, f32[2,6,512]{2,0,1:T(2,128)S(1)}, ...), condition=%wide.region_42.43_spmd, body=%wide.region_39.42_spmd.sunk | while | flops 159746 | bytes 639073 | solution.py:45
  343.9 17.8 %while.215 = (s32[]{:T(128)}, f32[2,6,512]{2,0,1:T(2,128)S(1)}, f32[2,6,512]{2,0,1:T(2,128)S(1)}, f32[8,2,6,6,512]{4,1,3,2,0:T(2,128)}, f32[8,2,6,6,512]{4,1,3,2...) while((s32[]{:T(128)}, f32[2,6,512]{2,0,1:T(2,128)S(1)}, ...), condition=%wide.region_47.48_spmd.clone, body=%wide.region_43.47_spmd.clone.sunk | while | flops 221188 | bytes 761991 | solution.py:60
  361.8 54.4 %while.210 = (s32[]{:T(128)}, f32[12,2,512]{2,1,0:T(2,128)S(1)}, f32[12,12,2,512]{3,2,1,0:T(2,128)S(1)}, f32[12,2,512]{2,1,0:T(2,128)S(1)}, s32[]{:T(128)}) while((s32[]{:T(128)}, f32[12,2,512]{2,1,0:T(2,128)S(1)}, f32[12,12,2,512]{3,2,1,0:T(2,128)S(1)}, f32[12,2,512]{2,1,0:T(2,128)S(1)}, s32[]{:T(128)}) %tuple.403), condition=%wide.region_49.50_spmd, body=%wide.region_48.49_spmd.sunk | while | flops 294914 | bytes 1032293 | solution.py:144
  363.4 6.5 %collective-permute-done.3 = f32[12,2,512]{2,1,0:T(2,128)S(1)} collective-permute-done((f32[12,2,512]{2,1,0:T(2,128)S(1)}, f32[12,2,512]{2,1,0:T(2,128)S(1)}, u32[]{:S(2)}, u32[]{:S(2)}) %collective-permute-start.3) | collective-permute-done | bytes 49184 | tf_op jit(solution)/shard_map/while/body/eval_jaxpr/ppermute | solution.py:26
  379.1 6.4 %collective-permute-done.3 = f32[12,2,512]{2,1,0:T(2,128)S(1)} collective-permute-done((f32[12,2,512]{2,1,0:T(2,128)S(1)}, f32[12,2,512]{2,1,0:T(2,128)S(1)}, u32[]{:S(2)}, u32[]{:S(2)}) %collective-permute-start.3) | collective-permute-done | bytes 49184 | tf_op jit(solution)/shard_map/while/body/eval_jaxpr/ppermute | solution.py:26
  387.0 6.2 %collective-permute-done.3 = f32[12,2,512]{2,1,0:T(2,128)S(1)} collective-permute-done((f32[12,2,512]{2,1,0:T(2,128)S(1)}, f32[12,2,512]{2,1,0:T(2,128)S(1)}, u32[]{:S(2)}, u32[]{:S(2)}) %collective-permute-start.3) | collective-permute-done | bytes 49184 | tf_op jit(solution)/shard_map/while/body/eval_jaxpr/ppermute | solution.py:26
  402.3 6.1 %collective-permute-done.3 = f32[12,2,512]{2,1,0:T(2,128)S(1)} collective-permute-done((f32[12,2,512]{2,1,0:T(2,128)S(1)}, f32[12,2,512]{2,1,0:T(2,128)S(1)}, u32[]{:S(2)}, u32[]{:S(2)}) %collective-permute-start.3) | collective-permute-done | bytes 49184 | tf_op jit(solution)/shard_map/while/body/eval_jaxpr/ppermute | solution.py:26
  410.0 6.2 %collective-permute-done.3 = f32[12,2,512]{2,1,0:T(2,128)S(1)} collective-permute-done((f32[12,2,512]{2,1,0:T(2,128)S(1)}, f32[12,2,512]{2,1,0:T(2,128)S(1)}, u32[]{:S(2)}, u32[]{:S(2)}) %collective-permute-start.3) | collective-permute-done | bytes 49184 | tf_op jit(solution)/shard_map/while/body/eval_jaxpr/ppermute | solution.py:26
  416.3 17.9 %while.211 = (s32[]{:T(128)}, f32[2,6,512]{2,0,1:T(2,128)S(1)}, f32[2,6,512]{2,0,1:T(2,128)S(1)}, f32[8,2,6,512]{3,1,2,0:T(2,128)S(1)}, f32[8,2,6,6,512]{4,1,3,2...) while((s32[]{:T(128)}, f32[2,6,512]{2,0,1:T(2,128)S(1)}, ...), condition=%wide.region_54.55_spmd, body=%wide.region_50.0_spmd.sunk | while | flops 215043 | bytes 811137 | solution.py:60
  435.6 12.2 %psum.7 = f32[8,3,512]{2,0,1:T(8,128)} all-reduce(f32[8,3,512]{2,0,1:T(8,128)S(1)} %bitcast.356), channel_id=1, replica_groups=mesh['cond'=2,'gx'=8,'gy'=16] {'cond'}, use_global_device_ids=true, to_apply=%region_56.57 | all-reduce | flops 12288 | bytes 98304 | tf_op jit(solution)/shard_map/psum | solution.py:159
  (602 shorter events, 373.9 us)
Async XLA Ops:
  2.2 86.9 %collective-permute-start.6 = (f32[8,2,6,32]{3,1,2,0:T(2,128)}, f32[8,2,6,32]{3,1,2,0:T(2,128)S(1)}, u32[]{:S(2)}, u32[]{:S(2)}) collective-permute-start(f32[8,2,6,32]{3,1,2,0:T(2,128)} %get-tuple-element.1343), channel_id=1, source_target_pairs={{1,0},{2,1},{3,2},{4,3},{5,4},{6,5},{7,6},{8,7},{9,8},{10,9},{11,1... | collective-permute-start | bytes 36872 | tf_op jit(solution)/shard_map/ppermute | solution.py:18
  4.1 85.0 %collective-permute-start.7 = (f32[8,2,6,32]{3,1,2,0:T(2,128)S(1)}, f32[8,2,6,32]{3,1,2,0:T(2,128)S(1)}, u32[]{:S(2)}, u32[]{:S(2)}) collective-permute-start(f32[8,2,6,32]{3,1,2,0:T(2,128)S(1)} %get-tuple-element.1344), channel_id=1, source_target_pairs={{0,1},{1,2},{2,3},{3,4},{4,5},{5,6},{6,7},{7,8},{8,9},{9,10},{10,1... | collective-permute-start | bytes 36872 | tf_op jit(solution)/shard_map/ppermute | solution.py:17
  7.9 81.3 %collective-permute-start.4 = (f32[1,2,6,512]{3,1,2,0:T(2,128)}, f32[1,2,6,512]{3,1,2,0:T(2,128)}, u32[]{:S(2)}, u32[]{:S(2)}) collective-permute-start(f32[1,2,6,512]{3,1,2,0:T(2,128)} %get-tuple-element.1341), channel_id=1, source_target_pairs={{16,0},{32,16},{48,32},{64,48},{80,64},{96,80},{112,96},{17,1},{33... | collective-permute-start | bytes 73736 | tf_op jit(solution)/shard_map/ppermute | solution.py:18
  9.1 80.0 %collective-permute-start.5 = (f32[1,2,6,512]{3,1,2,0:T(2,128)}, f32[1,2,6,512]{3,1,2,0:T(2,128)}, u32[]{:S(2)}, u32[]{:S(2)}) collective-permute-start(f32[1,2,6,512]{3,1,2,0:T(2,128)} %get-tuple-element.1342), channel_id=1, source_target_pairs={{0,16},{16,32},{32,48},{48,64},{64,80},{80,96},{96,112},{1,17},{17... | collective-permute-start | bytes 73736 | tf_op jit(solution)/shard_map/ppermute | solution.py:17
  137.5 7.2 %collective-permute-start = (f32[12,2,512]{2,1,0:T(2,128)S(1)}, f32[12,2,512]{2,1,0:T(2,128)S(1)}, u32[]{:S(2)}, u32[]{:S(2)}) collective-permute-start(f32[12,2,512]{2,1,0:T(2,128)S(1)} %bitcast_add_fusion.8), channel_id=1, source_target_pairs={{0,16},{16,32},{32,48},{48,64},{64,80},{80,96},{96,112},{1,17},{17... | collective-permute-start | bytes 147464 | tf_op jit(solution)/shard_map/while/body/eval_jaxpr/ppermute | solution.py:26
  145.0 7.2 %collective-permute-start = (f32[12,2,512]{2,1,0:T(2,128)S(1)}, f32[12,2,512]{2,1,0:T(2,128)S(1)}, u32[]{:S(2)}, u32[]{:S(2)}) collective-permute-start(f32[12,2,512]{2,1,0:T(2,128)S(1)} %bitcast_add_fusion.8), channel_id=1, source_target_pairs={{0,16},{16,32},{32,48},{48,64},{64,80},{80,96},{96,112},{1,17},{17... | collective-permute-start | bytes 147464 | tf_op jit(solution)/shard_map/while/body/eval_jaxpr/ppermute | solution.py:26
  179.8 7.8 %collective-permute-start.1 = (f32[12,2,512]{2,1,0:T(2,128)S(1)}, f32[12,2,512]{2,1,0:T(2,128)S(1)}, u32[]{:S(2)}, u32[]{:S(2)}) collective-permute-start(f32[12,2,512]{2,1,0:T(2,128)S(1)} %bitcast_add_fusion.9), channel_id=1, source_target_pairs={{16,0},{32,16},{48,32},{64,48},{80,64},{96,80},{112,96},{17,1},{33... | collective-permute-start | bytes 147464 | tf_op jit(solution)/shard_map/while/body/eval_jaxpr/ppermute | solution.py:26
  187.8 7.3 %collective-permute-start.1 = (f32[12,2,512]{2,1,0:T(2,128)S(1)}, f32[12,2,512]{2,1,0:T(2,128)S(1)}, u32[]{:S(2)}, u32[]{:S(2)}) collective-permute-start(f32[12,2,512]{2,1,0:T(2,128)S(1)} %bitcast_add_fusion.9), channel_id=1, source_target_pairs={{16,0},{32,16},{48,32},{64,48},{80,64},{96,80},{112,96},{17,1},{33... | collective-permute-start | bytes 147464 | tf_op jit(solution)/shard_map/while/body/eval_jaxpr/ppermute | solution.py:26
  195.4 7.5 %collective-permute-start.1 = (f32[12,2,512]{2,1,0:T(2,128)S(1)}, f32[12,2,512]{2,1,0:T(2,128)S(1)}, u32[]{:S(2)}, u32[]{:S(2)}) collective-permute-start(f32[12,2,512]{2,1,0:T(2,128)S(1)} %bitcast_add_fusion.9), channel_id=1, source_target_pairs={{16,0},{32,16},{48,32},{64,48},{80,64},{96,80},{112,96},{17,1},{33... | collective-permute-start | bytes 147464 | tf_op jit(solution)/shard_map/while/body/eval_jaxpr/ppermute | solution.py:26
  203.2 7.5 %collective-permute-start.1 = (f32[12,2,512]{2,1,0:T(2,128)S(1)}, f32[12,2,512]{2,1,0:T(2,128)S(1)}, u32[]{:S(2)}, u32[]{:S(2)}) collective-permute-start(f32[12,2,512]{2,1,0:T(2,128)S(1)} %bitcast_add_fusion.9), channel_id=1, source_target_pairs={{16,0},{32,16},{48,32},{64,48},{80,64},{96,80},{112,96},{17,1},{33... | collective-permute-start | bytes 147464 | tf_op jit(solution)/shard_map/while/body/eval_jaxpr/ppermute | solution.py:26
  251.7 12.5 %collective-permute-start.10 = (f32[8,2,6,32]{3,1,2,0:T(2,128)S(1)}, f32[8,2,6,32]{3,1,2,0:T(2,128)S(1)}, u32[]{:S(2)}, u32[]{:S(2)}) collective-permute-start(f32[8,2,6,32]{3,1,2,0:T(2,128)S(1)} %get-tuple-element.1339), channel_id=1, source_target_pairs={{1,0},{2,1},{3,2},{4,3},{5,4},{6,5},{7,6},{8,7},{9,8},{10,9},{11,1... | collective-permute-start | bytes 36872 | tf_op jit(solution)/shard_map/ppermute | solution.py:18
  253.6 10.5 %collective-permute-start.11 = (f32[8,2,6,32]{3,1,2,0:T(2,128)S(1)}, f32[8,2,6,32]{3,1,2,0:T(2,128)S(1)}, u32[]{:S(2)}, u32[]{:S(2)}) collective-permute-start(f32[8,2,6,32]{3,1,2,0:T(2,128)S(1)} %get-tuple-element.1340), channel_id=1, source_target_pairs={{0,1},{1,2},{2,3},{3,4},{4,5},{5,6},{6,7},{7,8},{8,9},{9,10},{10,1... | collective-permute-start | bytes 36872 | tf_op jit(solution)/shard_map/ppermute | solution.py:17
  256.1 8.1 %collective-permute-start.8 = (f32[1,2,6,512]{3,1,2,0:T(2,128)S(1)}, f32[1,2,6,512]{3,1,2,0:T(2,128)S(1)}, u32[]{:S(2)}, u32[]{:S(2)}) collective-permute-start(f32[1,2,6,512]{3,1,2,0:T(2,128)S(1)} %get-tuple-element.1337), channel_id=1, source_target_pairs={{16,0},{32,16},{48,32},{64,48},{80,64},{96,80},{112,96},{17,1},{33... | collective-permute-start | bytes 73736 | tf_op jit(solution)/shard_map/ppermute | solution.py:18
  257.4 7.5 %collective-permute-start.9 = (f32[1,2,6,512]{3,1,2,0:T(2,128)S(1)}, f32[1,2,6,512]{3,1,2,0:T(2,128)S(1)}, u32[]{:S(2)}, u32[]{:S(2)}) collective-permute-start(f32[1,2,6,512]{3,1,2,0:T(2,128)S(1)} %get-tuple-element.1338), channel_id=1, source_target_pairs={{0,16},{16,32},{32,48},{48,64},{64,80},{80,96},{96,112},{1,17},{17... | collective-permute-start | bytes 73736 | tf_op jit(solution)/shard_map/ppermute | solution.py:17
  304.6 7.3 %collective-permute-start.2 = (f32[12,2,512]{2,1,0:T(2,128)S(1)}, f32[12,2,512]{2,1,0:T(2,128)S(1)}, u32[]{:S(2)}, u32[]{:S(2)}) collective-permute-start(f32[12,2,512]{2,1,0:T(2,128)S(1)} %bitcast_add_fusion.10), channel_id=1, source_target_pairs={{0,16},{16,32},{32,48},{48,64},{64,80},{80,96},{96,112},{1,17},{17... | collective-permute-start | bytes 147464 | tf_op jit(solution)/shard_map/while/body/eval_jaxpr/ppermute | solution.py:26
  312.3 7.2 %collective-permute-start.2 = (f32[12,2,512]{2,1,0:T(2,128)S(1)}, f32[12,2,512]{2,1,0:T(2,128)S(1)}, u32[]{:S(2)}, u32[]{:S(2)}) collective-permute-start(f32[12,2,512]{2,1,0:T(2,128)S(1)} %bitcast_add_fusion.10), channel_id=1, source_target_pairs={{0,16},{16,32},{32,48},{48,64},{64,80},{80,96},{96,112},{1,17},{17... | collective-permute-start | bytes 147464 | tf_op jit(solution)/shard_map/while/body/eval_jaxpr/ppermute | solution.py:26
  319.8 7.2 %collective-permute-start.2 = (f32[12,2,512]{2,1,0:T(2,128)S(1)}, f32[12,2,512]{2,1,0:T(2,128)S(1)}, u32[]{:S(2)}, u32[]{:S(2)}) collective-permute-start(f32[12,2,512]{2,1,0:T(2,128)S(1)} %bitcast_add_fusion.10), channel_id=1, source_target_pairs={{0,16},{16,32},{32,48},{48,64},{64,80},{80,96},{96,112},{1,17},{17... | collective-permute-start | bytes 147464 | tf_op jit(solution)/shard_map/while/body/eval_jaxpr/ppermute | solution.py:26
  327.2 7.2 %collective-permute-start.2 = (f32[12,2,512]{2,1,0:T(2,128)S(1)}, f32[12,2,512]{2,1,0:T(2,128)S(1)}, u32[]{:S(2)}, u32[]{:S(2)}) collective-permute-start(f32[12,2,512]{2,1,0:T(2,128)S(1)} %bitcast_add_fusion.10), channel_id=1, source_target_pairs={{0,16},{16,32},{32,48},{48,64},{64,80},{80,96},{96,112},{1,17},{17... | collective-permute-start | bytes 147464 | tf_op jit(solution)/shard_map/while/body/eval_jaxpr/ppermute | solution.py:26
  362.1 7.8 %collective-permute-start.3 = (f32[12,2,512]{2,1,0:T(2,128)S(1)}, f32[12,2,512]{2,1,0:T(2,128)S(1)}, u32[]{:S(2)}, u32[]{:S(2)}) collective-permute-start(f32[12,2,512]{2,1,0:T(2,128)S(1)} %bitcast_add_fusion.11), channel_id=1, source_target_pairs={{16,0},{32,16},{48,32},{64,48},{80,64},{96,80},{112,96},{17,1},{33... | collective-permute-start | bytes 147464 | tf_op jit(solution)/shard_map/while/body/eval_jaxpr/ppermute | solution.py:26
  370.2 7.3 %collective-permute-start.3 = (f32[12,2,512]{2,1,0:T(2,128)S(1)}, f32[12,2,512]{2,1,0:T(2,128)S(1)}, u32[]{:S(2)}, u32[]{:S(2)}) collective-permute-start(f32[12,2,512]{2,1,0:T(2,128)S(1)} %bitcast_add_fusion.11), channel_id=1, source_target_pairs={{16,0},{32,16},{48,32},{64,48},{80,64},{96,80},{112,96},{17,1},{33... | collective-permute-start | bytes 147464 | tf_op jit(solution)/shard_map/while/body/eval_jaxpr/ppermute | solution.py:26
  377.8 7.7 %collective-permute-start.3 = (f32[12,2,512]{2,1,0:T(2,128)S(1)}, f32[12,2,512]{2,1,0:T(2,128)S(1)}, u32[]{:S(2)}, u32[]{:S(2)}) collective-permute-start(f32[12,2,512]{2,1,0:T(2,128)S(1)} %bitcast_add_fusion.11), channel_id=1, source_target_pairs={{16,0},{32,16},{48,32},{64,48},{80,64},{96,80},{112,96},{17,1},{33... | collective-permute-start | bytes 147464 | tf_op jit(solution)/shard_map/while/body/eval_jaxpr/ppermute | solution.py:26
  385.7 7.5 %collective-permute-start.3 = (f32[12,2,512]{2,1,0:T(2,128)S(1)}, f32[12,2,512]{2,1,0:T(2,128)S(1)}, u32[]{:S(2)}, u32[]{:S(2)}) collective-permute-start(f32[12,2,512]{2,1,0:T(2,128)S(1)} %bitcast_add_fusion.11), channel_id=1, source_target_pairs={{16,0},{32,16},{48,32},{64,48},{80,64},{96,80},{112,96},{17,1},{33... | collective-permute-start | bytes 147464 | tf_op jit(solution)/shard_map/while/body/eval_jaxpr/ppermute | solution.py:26
  401.0 7.4 %collective-permute-start.3 = (f32[12,2,512]{2,1,0:T(2,128)S(1)}, f32[12,2,512]{2,1,0:T(2,128)S(1)}, u32[]{:S(2)}, u32[]{:S(2)}) collective-permute-start(f32[12,2,512]{2,1,0:T(2,128)S(1)} %bitcast_add_fusion.11), channel_id=1, source_target_pairs={{16,0},{32,16},{48,32},{64,48},{80,64},{96,80},{112,96},{17,1},{33... | collective-permute-start | bytes 147464 | tf_op jit(solution)/shard_map/while/body/eval_jaxpr/ppermute | solution.py:26
  408.7 7.5 %collective-permute-start.3 = (f32[12,2,512]{2,1,0:T(2,128)S(1)}, f32[12,2,512]{2,1,0:T(2,128)S(1)}, u32[]{:S(2)}, u32[]{:S(2)}) collective-permute-start(f32[12,2,512]{2,1,0:T(2,128)S(1)} %bitcast_add_fusion.11), channel_id=1, source_target_pairs={{16,0},{32,16},{48,32},{64,48},{80,64},{96,80},{112,96},{17,1},{33... | collective-permute-start | bytes 147464 | tf_op jit(solution)/shard_map/while/body/eval_jaxpr/ppermute | solution.py:26
  (24 other events, 322.4 us)
where the time goes:
time: 457 us; the launch traced here: 448 us
  other arithmetic  165 us (36%)
  waiting for transfers between devices  111 us (24%)
  starting transfers between devices  110 us (24%)
  local copies, waits for them, and re-layouts  41.7 us (9%)
  blocking collectives  12.2 us (3%)
    ppermute x28, waiting for transfers between devices, from_behind(): lax.ppermute(value, axis, [(source, source + steps) for source in range(f...  110 us
    reduce_sum x82, other arithmetic, apply_transpose(): return jnp.sum(blocks * vector[..., :, None, :], axis=-3)  92 us
    ppermute x28, starting transfers between devices, from_behind(): lax.ppermute(value, axis, [(source, source + steps) for source in range(f...  87.8 us
    reduce_sum x40, other arithmetic, apply_block(): return jnp.sum(blocks * vector[..., None, :, :], axis=-2)  52.1 us
    mul x20, local copies, waits for them, and re-layouts, apply_transpose(): return jnp.sum(blocks * vector[..., :, None, :], axis=-3)  19.2 us
    ppermute x4, starting transfers between devices, extended(): before = lax.ppermute(last, axis, up)  16 us
    mul x16, local copies, waits for them, and re-layouts, apply_block(): return jnp.sum(blocks * vector[..., None, :, :], axis=-2)  14.8 us
    psum x1, blocking collectives, on_device(): mesh_sens = lax.psum(local_sens, 'cond')  12.2 us
  transfers between devices with their start and end apart: 36, of which 29 were waited for; matrix products, arithmetic and copies ran while one was open for 17% of the time, Pallas kernels for 0%

commit v1 on v0

v1 whole, which is shorter than its diff:
```python
import functools

import jax
import jax.numpy as jnp
from jax import lax
from jax.experimental import pallas as pl
from jax.experimental.pallas import tpu as pltpu
from jax.sharding import PartitionSpec as P

MESH = pl.DeviceIdType.MESH
F32 = jnp.float32
BF16 = jnp.bfloat16
NX = 8
ORDER = (4, 3, 5, 2, 6, 1, 7)


def pack(x):
    n = x.ndim
    y = jnp.transpose(x, (0,) + tuple(range(2, n - 1)) + (1, n - 1))
    s = y.shape[:-2]
    y = jnp.swapaxes(y.reshape(s + (2, 4, 128)), -3, -2)
    return y.reshape(s + (8, 128))


def unpack(y):
    s = y.shape[:-2]
    y = jnp.swapaxes(y.reshape(s + (4, 2, 128)), -3, -2).reshape(s + (2, 512))
    n = y.ndim
    return jnp.transpose(y, (0, n - 2) + tuple(range(1, n - 2)) + (n - 1,))


def kernel(
    psi_h, grad_h, nu_h, fu_h, inv_h, nl_h, fl_h, yi_h, zi_h, sens_h, mask_h, ci, wt,
    psi_o, ms_o,
    grad, nu, fu, inv, nl, fl, yi, zi, sens, mask,
    psi, hj, keep, weights, xs, zs, up, p0, og, ogr, own, ef,
    resp, pr_e, pr_f, st_n, st_q, diff, m_r, n_r, q_r, t2, t4, s2, s4, rolled, part_o, part_r,
    load_sem, bulk_s, bulk_r, small_s, small_r, halo_s, halo_r, own_sem, sum_sem,
):
    k = lax.axis_index("gx")
    g = lax.axis_index("gy")
    cond = lax.axis_index("cond")
    last_g = lax.axis_size("gy") - 1
    sub = lax.broadcasted_iota(jnp.int32, (8, 128), 0)
    lane = lax.broadcasted_iota(jnp.int32, (8, 128), 1)

    loads = {}
    for n, (name, src, dst) in enumerate((
        ("psi", psi_h, psi.at[0, 1:9]), ("nu", nu_h, nu), ("fu", fu_h, fu), ("inv", inv_h, inv),
        ("nl", nl_h, nl), ("fl", fl_h, fl), ("zi", zi_h, zi), ("grad", grad_h, grad),
        ("yi", yi_h, yi), ("mask", mask_h, mask), ("sens", sens_h, sens),
    )):
        loads[name] = pltpu.make_async_copy(src, dst, load_sem.at[n])
        loads[name].start()

    zero = jnp.zeros((8, 128), F32)
    one = jnp.ones((8, 128), F32)
    for it in range(2):
        psi[it, 0] = jnp.zeros((6, 8, 128), F32)
        psi[it, 9] = jnp.zeros((6, 8, 128), F32)

    def clear(i, _):
        hj[i] = jnp.zeros((2, 6, 8, 128), F32)
        return 0

    lax.fori_loop(0, 16, clear, 0)

    def clear_matrix(i, _):
        m_r[i] = jnp.zeros((12, 8, 128), F32)
        n_r[i] = jnp.zeros((12, 8, 128), F32)
        q_r[i] = jnp.zeros((12, 8, 128), F32)
        return 0

    lax.fori_loop(0, 12, clear_matrix, 0)
    for s in range(2):
        for v in range(6):
            for q in range(12):
                unit = one if q == 6 * s + v else zero
                resp[s, v, q] = unit
                st_n[s, v, q] = unit
                st_q[s, v, q] = zero

    barrier = pltpu.get_barrier_semaphore()
    for d in range(1, NX):
        pl.semaphore_signal(barrier, inc=1, device_id={"gx": lax.rem(k + d, NX)}, device_id_type=MESH)
    pl.semaphore_signal(barrier, inc=1, device_id={"cond": 1 - cond}, device_id_type=MESH)

    @pl.when(g > 0)
    def _():
        pl.semaphore_signal(barrier, inc=1, device_id={"gy": g - 1}, device_id_type=MESH)

    @pl.when(g < last_g)
    def _():
        pl.semaphore_signal(barrier, inc=1, device_id={"gy": g + 1}, device_id_type=MESH)

    neighbours = jnp.where(g > 0, 1, 0) + jnp.where(g < last_g, 1, 0)
    pl.semaphore_wait(barrier, NX + neighbours)

    def halo_copy(it, n):
        if n == 0:
            src, dst, to = psi.at[it, 8], psi.at[it, 0], {"gx": lax.rem(k + 1, NX)}
        elif n == 1:
            src, dst, to = psi.at[it, 1], psi.at[it, 9], {"gx": lax.rem(k + NX - 1, NX)}
        elif n == 2:
            src, dst, to = psi.at[it, 1:9, :, 6:8], hj.at[pl.ds(it * 8, 8), 0, :, 0:2], {"gy": lax.rem(g + 1, last_g + 1)}
        else:
            src, dst, to = psi.at[it, 1:9, :, 0:2], hj.at[pl.ds(it * 8, 8), 1, :, 6:8], {"gy": lax.rem(g + last_g, last_g + 1)}
        return pltpu.make_async_remote_copy(
            src_ref=src, dst_ref=dst, send_sem=halo_s.at[it, n], recv_sem=halo_r.at[it, n],
            device_id=to, device_id_type=MESH)

    sends = (k < NX - 1, k > 0, g < last_g, g > 0)
    takes = (k > 0, k < NX - 1, g > 0, g < last_g)

    def halo_start(it, which):
        for n in which:
            @pl.when(sends[n])
            def _(n=n):
                halo_copy(it, n).start()

    def halo_wait(it):
        for n in range(4):
            @pl.when(takes[n])
            def _(n=n):
                halo_copy(it, n).wait_recv()

    def halo_drain(it):
        for n in range(4):
            @pl.when(sends[n])
            def _(n=n):
                halo_copy(it, n).wait_send()

    bulk = (
        (resp.at[8:10], m_r, lambda x: (x > 0) & (x < NX - 1), 1),
        (st_n, n_r, lambda x: (x > 0) & (x < NX - 1), -1),
        (st_q, q_r, lambda x: x > 0, -1),
    )

    def bulk_copy(n, d, source):
        src, dst, _, move = bulk[n]
        to = lax.rem(source + d, NX)
        row = lax.rem(source + NX + move, NX)
        return pltpu.make_async_remote_copy(
            src_ref=src.at[:, :, :, to], dst_ref=dst.reshape(2, 6, 12, 8, 128).at[:, :, :, row],
            send_sem=bulk_s.at[n, d], recv_sem=bulk_r.at[n, d],
            device_id={"gx": to}, device_id_type=MESH)

    def bulk_own(n):
        src, dst, _, move = bulk[n]
        row = lax.rem(k + NX + move, NX)
        return pltpu.make_async_copy(
            src.at[:, :, :, k], dst.reshape(2, 6, 12, 8, 128).at[:, :, :, row], own_sem.at[n])

    def bulk_start(n):
        @pl.when(bulk[n][2](k))
        def _():
            for d in ORDER:
                bulk_copy(n, d, k).start()
            bulk_own(n).start()

    def bulk_wait(n):
        for d in ORDER:
            source = lax.rem(k + NX - d, NX)

            @pl.when(bulk[n][2](source))
            def _(d=d, source=source):
                bulk_copy(n, d, source).wait_recv()

        @pl.when(bulk[n][2](k))
        def _():
            bulk_own(n).wait()

    def bulk_drain(n):
        @pl.when(bulk[n][2](k))
        def _():
            for d in ORDER:
                bulk_copy(n, d, k).wait_send()

    def small_copy(it, back, d, source):
        src, dst = (own, ef) if back else (og, ogr)
        to = lax.rem(source + d, NX)
        return pltpu.make_async_remote_copy(
            src_ref=src.at[it, :, to], dst_ref=dst.at[it, :, source],
            send_sem=small_s.at[2 * it + back, d], recv_sem=small_r.at[2 * it + back, d],
            device_id={"gx": to}, device_id_type=MESH)

    def small_exchange(it, back):
        src, dst = (own, ef) if back else (og, ogr)
        for d in ORDER:
            small_copy(it, back, d, k).start()
        mine = pltpu.make_async_copy(src.at[it, :, k], dst.at[it, :, k], own_sem.at[3 + 2 * it + back])
        mine.start()
        return mine

    def small_wait(it, back, mine):
        for d in ORDER:
            small_copy(it, back, d, lax.rem(k + NX - d, NX)).wait_recv()
        mine.wait()

    def small_drain(it, back):
        for d in ORDER:
            small_copy(it, back, d, k).wait_send()

    def upper_response(i, _):
        for w in range(0, 6, 2):
            acc = jnp.zeros((2, 12, 8, 128), F32)
            for v in range(6):
                acc += nu[i, w:w + 2, v][:, None] * resp[i + 1, v][None]
                acc += fu[i, w:w + 2, v][:, None] * resp[i, v][None]
            resp[i + 2, w:w + 2] = -acc
        return 0

    def lower_response(state, out, with_upper, t, _):
        i = NX - 1 - t
        for v in range(6):
            if with_upper:
                diff[v] = resp[i + 2, v] - state[0, v]
            else:
                diff[v] = -state[0, v]
        for w in range(0, 6, 2):
            acc = jnp.zeros((2, 12, 8, 128), F32)
            for v in range(6):
                acc += inv[i, v, w:w + 2][:, None] * diff[v][None]
            out[i, w:w + 2] = acc
        for w in range(0, 6, 2):
            near = state[1, w:w + 2]
            far = jnp.zeros((2, 12, 8, 128), F32)
            for v in range(6):
                p = out[i, v][None]
                near += nl[i, v, w:w + 2][:, None] * p
                far += fl[i, v, w:w + 2][:, None] * p
            state[0, w:w + 2] = near
            state[1, w:w + 2] = far
        return 0

    def local(it):
        halo_wait(it)
        for i in range(NX):
            here = psi[it, i + 1]
            down = pltpu.roll(here, 2, 1)
            down = jnp.where(sub < 2, hj[it * 8 + i, 0], down)
            down = pltpu.roll(jnp.where(lane >= 96, down, here), 32, 2)
            above = pltpu.roll(here, 6, 1)
            above = jnp.where(sub >= 6, hj[it * 8 + i, 1], above)
            above = pltpu.roll(jnp.where(lane < 32, above, here), 96, 2)
            beside = psi[it, i] + psi[it, i + 2] + down + above
            xs[:, i] = grad[i] + 0.5 * beside - 2.0 * here
        for v in range(6):
            x = xs[v].reshape(64, 128)
            hi = x.astype(BF16)
            lo = (x - hi.astype(F32)).astype(BF16)
            both = jnp.concatenate(
                [jnp.concatenate([hi, hi], axis=1), jnp.concatenate([lo, lo], axis=1)], axis=0)
            r = jnp.dot(both, weights[v], preferred_element_type=F32)
            r = (r[:64] + r[64:]).reshape(8, 8, 256)
            zs[v] = jnp.where(sub % 2 == 0, r[:, :, :128], r[:, :, 128:])
        last = jnp.zeros((6, 8, 128), F32)
        before = jnp.zeros((6, 8, 128), F32)
        for i in range(NX):
            now = jnp.zeros((6, 8, 128), F32)
            for v in range(6):
                now += yi[i, v] * zs[v, i]
            for v in range(6):
                now -= fu[i, :, v] * before[v]
            for v in range(6):
                now -= nu[i, :, v] * last[v]
            up[i] = now
            last, before = now, last
        og[it, 0:6] = before
        og[it, 6:12] = last
        pending = jnp.zeros((6, 8, 128), F32)
        partial = jnp.zeros((6, 8, 128), F32)
        for i in range(NX - 1, -1, -1):
            d = up[i] - pending
            p = jnp.zeros((6, 8, 128), F32)
            for v in range(6):
                p += inv[i, v] * d[v]
            p0[i] = p
            pending = partial
            partial = jnp.zeros((6, 8, 128), F32)
            for v in range(6):
                pending += nl[i, v] * p[v]
                partial += fl[i, v] * p[v]
        og[it, 12:18] = pending
        og[it, 18:24] = partial

    def product(dst, a, b, shift):
        def turn(q, _):
            rolled[q] = pltpu.roll(b[q], shift, 1)
            return 0

        lax.fori_loop(0, 12, turn, 0)

        def rows(m, _):
            acc = jnp.zeros((2, 12, 8, 128), F32)
            for q in range(12):
                acc += a[pl.ds(2 * m, 2), q][:, None] * rolled[q][None]
            dst[pl.ds(2 * m, 2)] = acc
            return 0

        lax.fori_loop(0, 6, rows, 0)

    def apply(x, a, by, shift):
        turned = pltpu.roll(by, shift, 1)
        for q in range(12):
            x = x + a[:, q] * turned[q]
        return x

    def owner(it):
        u = jnp.where(sub == 0, 0.0, pltpu.roll(ogr[it, 0:12], 1, 1))
        u = apply(u, m_r, u, 1)
        u = apply(u, t2, u, 2)
        u = apply(u, t4, u, 4)
        own[it, 0:12] = u
        w = jnp.where(sub == 7, 0.0, pltpu.roll(ogr[it, 12:24], 7, 1))
        w = apply(w, q_r, u, 7)
        w = apply(w, n_r, w, 7)
        w = apply(w, s2, w, 6)
        w = apply(w, s4, w, 4)
        own[it, 12:24] = w

    def solved(it, i):
        p = p0[i]
        for q in range(12):
            p += pr_e[i, :, q] * ef[it, q]
        for q in range(12):
            p += pr_f[i, :, q] * ef[it, 12 + q]
        return (psi[it, i + 1] + 0.05 * p) * keep[i]

    loads["psi"].wait()
    halo_start(0, range(4))
    loads["nu"].wait()
    loads["fu"].wait()
    lax.fori_loop(0, NX, upper_response, 0)
    bulk_start(0)
    loads["inv"].wait()
    loads["nl"].wait()
    loads["fl"].wait()
    lax.fori_loop(0, NX, functools.partial(lower_response, st_n, pr_f, False), 0)
    bulk_start(1)
    lax.fori_loop(0, NX, functools.partial(lower_response, st_q, pr_e, True), 0)
    bulk_start(2)

    loads["zi"].wait()
    z = zi[...].reshape(2 * 6 * 32, 32)
    z_hi = z.astype(BF16)
    z_lo = (z - z_hi.astype(F32)).astype(BF16)
    spread = (
        lax.broadcasted_iota(jnp.int32, (32, 128), 1) % 32 == lax.broadcasted_iota(jnp.int32, (32, 128), 0)
    ).astype(F32).astype(BF16)
    lane32 = lax.broadcasted_iota(jnp.int32, (32, 128), 1) // 32
    for half, part in enumerate((z_hi, z_lo)):
        tiled = jnp.dot(part, spread, preferred_element_type=F32)
        for c in range(2):
            for v in range(6):
                at = (c * 6 + v) * 32
                rows = tiled[at:at + 32]
                for b in range(4):
                    weights[v, half * 128 + b * 32:half * 128 + b * 32 + 32, c * 128:c * 128 + 128] = (
                        jnp.where(lane32 == b, rows, 0.0).astype(BF16))
    loads["mask"].wait()
    open_cells = 1.0 - mask[...].astype(F32)
    for i in range(NX):
        row = jnp.zeros((8, 128), F32)
        for j in range(4):
            row = jnp.where(sub // 2 == j, open_cells[i:i + 1, j * 128:j * 128 + 128], row)
        keep[i] = row

    loads["grad"].wait()
    loads["yi"].wait()
    local(0)
    mine = small_exchange(0, 0)
    bulk_wait(0)
    product(t2, m_r, m_r, 1)
    product(t4, t2, t2, 2)
    bulk_wait(1)
    product(s2, n_r, n_r, 7)
    product(s4, s2, s2, 6)
    bulk_wait(2)
    small_wait(0, 0, mine)
    owner(0)
    mine = small_exchange(0, 1)
    small_wait(0, 1, mine)
    for i in (7, 0):
        psi[1, i + 1] = solved(0, i)
    halo_start(1, (0, 1))
    for i in range(1, 7):
        psi[1, i + 1] = solved(0, i)
    halo_start(1, (2, 3))
    local(1)
    mine = small_exchange(1, 0)
    small_wait(1, 0, mine)
    owner(1)
    mine = small_exchange(1, 1)
    loads["sens"].wait()
    factor = []
    for c in range(2):
        value = 0.0
        for n in range(8):
            value = value + jnp.where(ci[c] == n, wt[n], 0.0)
        factor.append(value)
    weight = jnp.where(sub % 2 == 0, factor[0], factor[1])
    small_wait(1, 1, mine)
    tiles = [[jnp.zeros((8, 128), F32) for _ in range(4)] for _ in range(3)]
    for i in range(NX):
        new = solved(1, i)
        psi_o[i] = new
        new = new * weight
        for m in range(3):
            total = jnp.zeros((8, 128), F32)
            for v in range(6):
                total += new[v] * sens[i, m, v]
            total += pltpu.roll(total, 7, 0)
            for j in range(4):
                shift = (i - 2 * j) % 8
                turned = pltpu.roll(total, shift, 0) if shift else total
                tiles[m][j] = jnp.where(sub == i, turned, tiles[m][j])
    for m in range(3):
        for j in range(4):
            part_o[m, :, j * 128:j * 128 + 128] = tiles[m][j]
    across = pltpu.make_async_remote_copy(
        src_ref=part_o, dst_ref=part_r, send_sem=sum_sem.at[0], recv_sem=sum_sem.at[1],
        device_id={"cond": 1 - cond}, device_id_type=MESH)
    across.start()
    for n in range(3):
        bulk_drain(n)
    for it in range(2):
        halo_drain(it)
        small_drain(it, 0)
        small_drain(it, 1)
    across.wait()
    ms_o[...] = part_o[...] + part_r[...]


def on_device(
    psi_old, objective_grad, near_upper, far_upper, inverse_diag, near_lower, far_lower,
    y_inverse, z_inverse, sens_terms, wall_mask, cond_index, weight_table,
):
    cell = (8, 6, 8, 128)
    block = (8, 6, 6, 8, 128)
    matrix = (12, 12, 8, 128)
    vm = lambda *shape: pltpu.VMEM(shape, F32)
    dma = pltpu.SemaphoreType.DMA
    far = pl.BlockSpec(memory_space=pl.ANY)
    scalars = pl.BlockSpec(memory_space=pltpu.SMEM)
    near = pl.BlockSpec(memory_space=pltpu.VMEM)
    psi, sens = pl.pallas_call(
        kernel,
        name="adjoint",
        out_shape=(jax.ShapeDtypeStruct(cell, F32), jax.ShapeDtypeStruct((3, 8, 512), F32)),
        in_specs=[far] * 11 + [scalars] * 2,
        out_specs=(near, near),
        scratch_shapes=[
            vm(*cell), vm(*block), vm(*block), vm(*block), vm(*block), vm(*block), vm(*block),
            vm(2, 6, 32, 32), vm(8, 3, 6, 8, 128), pltpu.VMEM((8, 512), jnp.int32),
            vm(2, 10, 6, 8, 128), vm(16, 2, 6, 8, 128), vm(8, 8, 128), pltpu.VMEM((6, 256, 256), BF16),
            vm(6, 8, 8, 128), vm(6, 8, 8, 128), vm(*cell), vm(*cell),
            vm(2, 24, 8, 128), vm(2, 24, 8, 128), vm(2, 24, 8, 128), vm(2, 24, 8, 128),
            vm(10, 6, 12, 8, 128), vm(8, 6, 12, 8, 128), vm(8, 6, 12, 8, 128),
            vm(2, 6, 12, 8, 128), vm(2, 6, 12, 8, 128), vm(6, 12, 8, 128),
            vm(*matrix), vm(*matrix), vm(*matrix), vm(*matrix), vm(*matrix), vm(*matrix), vm(*matrix), vm(*matrix),
            vm(3, 8, 512), vm(3, 8, 512),
            dma((11,)), dma((3, 8)), dma((3, 8)), dma((4, 8)), dma((4, 8)), dma((2, 4)), dma((2, 4)),
            dma((7,)), dma((2,)),
        ],
        compiler_params=pltpu.CompilerParams(
            collective_id=0, has_side_effects=True, vmem_limit_bytes=58 * 2**20),
        cost_estimate=pl.CostEstimate(flops=10**8, bytes_accessed=9 * 10**6, transcendentals=0),
    )(
        pack(psi_old), pack(objective_grad), pack(near_upper), pack(far_upper), pack(inverse_diag),
        pack(near_lower), pack(far_lower), pack(y_inverse), z_inverse, pack(sens_terms),
        wall_mask, cond_index, weight_table,
    )
    return unpack(psi), jnp.transpose(sens, (1, 0, 2))


def solution(mesh):
    cell = P("gx", "cond", None, "gy")
    block = P("gx", "cond", None, None, "gy")
    placed = (
        cell, cell, block, block, block, block, block, block,
        P("cond", None, None, None), block, P("gx", "gy"), P("cond"), P(),
    )
    return jax.shard_map(
        on_device, mesh=mesh, in_specs=placed, out_specs=(cell, P("gx", None, "gy")), check_vma=False)
```

time: 457 us -> 84.6 us (0.19); the launches traced: 448 us -> 84.4 us
  other arithmetic: 165 us -> 0 us
  waiting for transfers between devices: 111 us -> 0 us
  starting transfers between devices: 110 us -> 0 us
  Pallas kernels: 0 us -> 80.7 us
  local copies, waits for them, and re-layouts: 41.7 us -> 3.04 us
  blocking collectives: 12.2 us -> 0 us
    reduce_sum x123 -> x0, other arithmetic: 145 us -> none  [the longest x82 92 us: apply_transpose(): return jnp.sum(blocks * vector[..., :, None, :], axis=-3)]
    ppermute x36 -> x0, waiting for transfers between devices: 111 us -> none  [the longest x28 110 us: from_behind(): lax.ppermute(value, axis, [(source, source + steps) for source in range(f...]
    ppermute x36 -> x0, starting transfers between devices: 110 us -> none  [the longest x28 87.8 us: from_behind(): lax.ppermute(value, axis, [(source, source + steps) for source in range(f...]
    pallas_call x0 -> x1, Pallas kernels: none -> 80.7 us  [on_device(): pl.pallas_call(kernel, name='adjoint', out_shape=(jax.ShapeDtypeStruct(ce...]
    mul x36 -> x0, local copies, waits for them, and re-layouts: 34 us -> none  [the longest x20 19.2 us: apply_transpose(): return jnp.sum(blocks * vector[..., :, None, :], axis=-3)]
    psum x1 -> x0, blocking collectives: 12.2 us -> none  [on_device(): mesh_sens = lax.psum(local_sens, 'cond')]
    sub x83 -> x0, other arithmetic: 7.46 us -> none  [the longest x2 3.41 us: on_device(): rhs = objective_grad + 0.5 * beside_all - 2.0 * psi]
    dot_general x28 -> x0, other arithmetic: 7.1 us -> none  [carry_through(): jnp.einsum('kcl,kmcl->mcl', vector, matrix, precision=lax.Precision.HIGHEST)]
  transfers between devices with their start and end apart: 36 -> 0, of which waited for: 29 -> 0; matrix products, arithmetic and copies ran while one was open for 17% -> 0% of each run, Pallas kernels for 0% -> 0%
where the time goes in v1:
time: 84.6 us; the launch traced here: 84.4 us
  Pallas kernels  80.7 us (95%)
  local copies, waits for them, and re-layouts  3.04 us (4%)
    pallas_call x1, Pallas kernels, on_device(): pl.pallas_call(kernel, name='adjoint', out_shape=(jax.ShapeDtypeStruct(ce...  80.7 us
    unnamed x2, local copies, waits for them, and re-layouts  3.04 us

profile of v1, /device:TPU:8, one launch (start us, length us, event | category | flops | bytes accessed | tf_op | source)
XLA Modules:
  0.0 84.4 jit_solution(6576488299297666002)
XLA Ops:
  0.6 80.7 %adjoint.1 = (f32[8,6,8,128]{3,2,1,0:T(8,128)}, f32[3,8,512]{2,1,0:T(8,128)}) custom-call(f32[8,6,8,128]{3,2,1,0:T(8,128)} %bitcast.79, f32[8,6,8,128]{3,2,1,0:T(8,128)} %bitcast.80, f32[8,6,6,8,128]{4,3,2,1,0:T(8,128)} %bitcast.71, f32[8,6,6,8,128]{4,3,2,1,0:T(8,128)} %bitcast.72, f32[8,6,6,8,128]{4,3,2,1,0:T(8,128)} %bitcast.73, ...), custom_call_target="tpu_custom_call" | custom-call | flops 100000000 | bytes 9000000 | tf_op jit(solution)/shard_map/adjoint/pallas_call | solution.py:447
  81.4 1.6 %copy.26 = f32[8,2,6,512]{3,1,2,0:T(2,128)} copy(f32[8,2,6,512]{3,1,2,0:T(2,128)} %bitcast.78) | data formatting | bytes 393216
  83.0 1.4 %copy.27 = f32[8,3,512]{2,0,1:T(8,128)} copy(f32[8,3,512]{2,0,1:T(8,128)} %bitcast.81) | data formatting | bytes 98304

commit v2 on v1

--- a/solution.py
+++ b/solution.py
@@ -46,12 +46,13 @@
 
     loads = {}
     for n, (name, src, dst) in enumerate((
-        ("psi", psi_h, psi.at[0, 1:9]), ("nu", nu_h, nu), ("fu", fu_h, fu), ("inv", inv_h, inv),
+        ("nu", nu_h, nu), ("fu", fu_h, fu), ("psi", psi_h, psi.at[0, 1:9]), ("inv", inv_h, inv),
         ("nl", nl_h, nl), ("fl", fl_h, fl), ("zi", zi_h, zi), ("grad", grad_h, grad),
         ("yi", yi_h, yi), ("mask", mask_h, mask), ("sens", sens_h, sens),
     )):
         loads[name] = pltpu.make_async_copy(src, dst, load_sem.at[n])
-        loads[name].start()
+        if n < 3:
+            loads[name].start()
 
     zero = jnp.zeros((8, 128), F32)
     one = jnp.ones((8, 128), F32)
@@ -72,13 +73,6 @@
         return 0
 
     lax.fori_loop(0, 12, clear_matrix, 0)
-    for s in range(2):
-        for v in range(6):
-            for q in range(12):
-                unit = one if q == 6 * s + v else zero
-                resp[s, v, q] = unit
-                st_n[s, v, q] = unit
-                st_q[s, v, q] = zero
 
     barrier = pltpu.get_barrier_semaphore()
     for d in range(1, NX):
@@ -92,9 +86,6 @@
     @pl.when(g < last_g)
     def _():
         pl.semaphore_signal(barrier, inc=1, device_id={"gy": g + 1}, device_id_type=MESH)
-
-    neighbours = jnp.where(g > 0, 1, 0) + jnp.where(g < last_g, 1, 0)
-    pl.semaphore_wait(barrier, NX + neighbours)
 
     def halo_copy(it, n):
         if n == 0:
@@ -131,40 +122,42 @@
                 halo_copy(it, n).wait_send()
 
     bulk = (
-        (resp.at[8:10], m_r, lambda x: (x > 0) & (x < NX - 1), 1),
-        (st_n, n_r, lambda x: (x > 0) & (x < NX - 1), -1),
-        (st_q, q_r, lambda x: x > 0, -1),
+        (resp.reshape(720, 8, 128).at[576:720], m_r, lambda x: (x > 0) & (x < NX - 1), 1, (0, 144), 0),
+        (st_n.reshape(144, 8, 128), n_r, lambda x: (x > 0) & (x < NX - 1), -1, (0, 48, 96, 144), 1),
+        (st_q.reshape(144, 8, 128), q_r, lambda x: x > 0, -1, (0, 48, 108, 144), 4),
     )
 
-    def bulk_copy(n, d, source):
-        src, dst, _, move = bulk[n]
+    def bulk_copy(n, d, source, part):
+        src, dst, _, move, cuts, first = bulk[n]
         to = lax.rem(source + d, NX)
         row = lax.rem(source + NX + move, NX)
+        span = slice(cuts[part], cuts[part + 1])
         return pltpu.make_async_remote_copy(
-            src_ref=src.at[:, :, :, to], dst_ref=dst.reshape(2, 6, 12, 8, 128).at[:, :, :, row],
-            send_sem=bulk_s.at[n, d], recv_sem=bulk_r.at[n, d],
+            src_ref=src.at[span, to], dst_ref=dst.reshape(144, 8, 128).at[span, row],
+            send_sem=bulk_s.at[first + part, d], recv_sem=bulk_r.at[first + part, d],
             device_id={"gx": to}, device_id_type=MESH)
 
     def bulk_own(n):
-        src, dst, _, move = bulk[n]
+        src, dst, _, move, _, _ = bulk[n]
         row = lax.rem(k + NX + move, NX)
-        return pltpu.make_async_copy(
-            src.at[:, :, :, k], dst.reshape(2, 6, 12, 8, 128).at[:, :, :, row], own_sem.at[n])
-
-    def bulk_start(n):
+        return pltpu.make_async_copy(src.at[:, k], dst.reshape(144, 8, 128).at[:, row], own_sem.at[n])
+
+    def bulk_start(n, part=0):
         @pl.when(bulk[n][2](k))
         def _():
             for d in ORDER:
-                bulk_copy(n, d, k).start()
-            bulk_own(n).start()
+                bulk_copy(n, d, k, part).start()
+            if part == 0:
+                bulk_own(n).start()
 
     def bulk_wait(n):
-        for d in ORDER:
-            source = lax.rem(k + NX - d, NX)
-
-            @pl.when(bulk[n][2](source))
-            def _(d=d, source=source):
-                bulk_copy(n, d, source).wait_recv()
+        for part in range(len(bulk[n][4]) - 1):
+            for d in ORDER:
+                source = lax.rem(k + NX - d, NX)
+
+                @pl.when(bulk[n][2](source))
+                def _(d=d, source=source, part=part):
+                    bulk_copy(n, d, source, part).wait_recv()
 
         @pl.when(bulk[n][2](k))
         def _():
@@ -173,33 +166,39 @@
     def bulk_drain(n):
         @pl.when(bulk[n][2](k))
         def _():
-            for d in ORDER:
-                bulk_copy(n, d, k).wait_send()
-
-    def small_copy(it, back, d, source):
+            for part in range(len(bulk[n][4]) - 1):
+                for d in ORDER:
+                    bulk_copy(n, d, k, part).wait_send()
+
+    small = ((0, 0, 0, 12), (0, 1, 0, 12), (0, 0, 12, 24), (0, 1, 12, 24), (1, 0, 0, 24), (1, 1, 0, 24))
+
+    def small_copy(n, d, source):
+        it, back, first, end = small[n]
         src, dst = (own, ef) if back else (og, ogr)
         to = lax.rem(source + d, NX)
         return pltpu.make_async_remote_copy(
-            src_ref=src.at[it, :, to], dst_ref=dst.at[it, :, source],
-            send_sem=small_s.at[2 * it + back, d], recv_sem=small_r.at[2 * it + back, d],
+            src_ref=src.at[it, first:end, to], dst_ref=dst.at[it, first:end, source],
+            send_sem=small_s.at[n, d], recv_sem=small_r.at[n, d],
             device_id={"gx": to}, device_id_type=MESH)
 
-    def small_exchange(it, back):
+    def small_own(n):
+        it, back, first, end = small[n]
         src, dst = (own, ef) if back else (og, ogr)
+        return pltpu.make_async_copy(src.at[it, first:end, k], dst.at[it, first:end, k], own_sem.at[3 + n])
+
+    def small_start(n):
         for d in ORDER:
-            small_copy(it, back, d, k).start()
-        mine = pltpu.make_async_copy(src.at[it, :, k], dst.at[it, :, k], own_sem.at[3 + 2 * it + back])
-        mine.start()
-        return mine
-
-    def small_wait(it, back, mine):
+            small_copy(n, d, k).start()
+        small_own(n).start()
+
+    def small_wait(n):
         for d in ORDER:
-            small_copy(it, back, d, lax.rem(k + NX - d, NX)).wait_recv()
-        mine.wait()
-
-    def small_drain(it, back):
+            small_copy(n, d, lax.rem(k + NX - d, NX)).wait_recv()
+        small_own(n).wait()
+
+    def small_drain(n):
         for d in ORDER:
-            small_copy(it, back, d, k).wait_send()
+            small_copy(n, d, k).wait_send()
 
     def upper_response(i, _):
         for w in range(0, 6, 2):
@@ -306,17 +305,29 @@
             x = x + a[:, q] * turned[q]
         return x
 
-    def owner(it):
+    def steps(x, a, shift):
+        return lax.fori_loop(0, NX - 2, lambda _, y: apply(x, a, y, shift), x)
+
+    def owner_upper(it):
         u = jnp.where(sub == 0, 0.0, pltpu.roll(ogr[it, 0:12], 1, 1))
-        u = apply(u, m_r, u, 1)
-        u = apply(u, t2, u, 2)
-        u = apply(u, t4, u, 4)
+        if it == 0:
+            u = steps(u, m_r, 1)
+        else:
+            u = apply(u, m_r, u, 1)
+            u = apply(u, t2, u, 2)
+            u = apply(u, t4, u, 4)
         own[it, 0:12] = u
+        return u
+
+    def owner_lower(it, u):
         w = jnp.where(sub == 7, 0.0, pltpu.roll(ogr[it, 12:24], 7, 1))
-        w = apply(w, q_r, u, 7)
-        w = apply(w, n_r, w, 7)
-        w = apply(w, s2, w, 6)
-        w = apply(w, s4, w, 4)
+        if it == 0:
+            w = steps(w, n_r, 7)
+        else:
+            w = apply(w, q_r, u, 7)
+            w = apply(w, n_r, w, 7)
+            w = apply(w, s2, w, 6)
+            w = apply(w, s4, w, 4)
         own[it, 12:24] = w
 
     def solved(it, i):
@@ -327,19 +338,29 @@
             p += pr_f[i, :, q] * ef[it, 12 + q]
         return (psi[it, i + 1] + 0.05 * p) * keep[i]
 
-    loads["psi"].wait()
-    halo_start(0, range(4))
+    for s in range(2):
+        for v in range(6):
+            for q in range(12):
+                unit = one if q == 6 * s + v else zero
+                resp[s, v, q] = unit
+                st_n[s, v, q] = unit
+                st_q[s, v, q] = zero
+
     loads["nu"].wait()
     loads["fu"].wait()
+    for name in ("inv", "nl", "fl", "zi", "grad", "yi", "mask", "sens"):
+        loads[name].start()
     lax.fori_loop(0, NX, upper_response, 0)
+    loads["psi"].wait()
+    neighbours = jnp.where(g > 0, 1, 0) + jnp.where(g < last_g, 1, 0)
+    pl.semaphore_wait(barrier, NX + neighbours)
+    halo_start(0, range(4))
     bulk_start(0)
     loads["inv"].wait()
     loads["nl"].wait()
     loads["fl"].wait()
     lax.fori_loop(0, NX, functools.partial(lower_response, st_n, pr_f, False), 0)
-    bulk_start(1)
     lax.fori_loop(0, NX, functools.partial(lower_response, st_q, pr_e, True), 0)
-    bulk_start(2)
 
     loads["zi"].wait()
     z = zi[...].reshape(2 * 6 * 32, 32)
@@ -369,29 +390,44 @@
     loads["grad"].wait()
     loads["yi"].wait()
     local(0)
-    mine = small_exchange(0, 0)
+    small_start(0)
+    bulk_start(1, 0)
     bulk_wait(0)
+    small_wait(0)
+    owner_upper(0)
+    small_start(1)
+    bulk_start(1, 1)
     product(t2, m_r, m_r, 1)
     product(t4, t2, t2, 2)
+    small_wait(1)
+    offset = og[0, 12:24]
+    for q in range(12):
+        offset += st_q.reshape(12, 12, 8, 128)[:, q] * ef[0, q]
+    og[0, 12:24] = offset
+    small_start(2)
+    bulk_start(1, 2)
+    bulk_start(2, 0)
     bulk_wait(1)
+    small_wait(2)
+    owner_lower(0, None)
+    small_start(3)
+    bulk_start(2, 1)
     product(s2, n_r, n_r, 7)
     product(s4, s2, s2, 6)
-    bulk_wait(2)
-    small_wait(0, 0, mine)
-    owner(0)
-    mine = small_exchange(0, 1)
-    small_wait(0, 1, mine)
+    small_wait(3)
     for i in (7, 0):
         psi[1, i + 1] = solved(0, i)
     halo_start(1, (0, 1))
     for i in range(1, 7):
         psi[1, i + 1] = solved(0, i)
     halo_start(1, (2, 3))
+    bulk_start(2, 2)
     local(1)
-    mine = small_exchange(1, 0)
-    small_wait(1, 0, mine)
-    owner(1)
-    mine = small_exchange(1, 1)
+    small_start(4)
+    bulk_wait(2)
+    small_wait(4)
+    owner_lower(1, owner_upper(1))
+    small_start(5)
     loads["sens"].wait()
     factor = []
     for c in range(2):
@@ -400,7 +436,7 @@
             value = value + jnp.where(ci[c] == n, wt[n], 0.0)
         factor.append(value)
     weight = jnp.where(sub % 2 == 0, factor[0], factor[1])
-    small_wait(1, 1, mine)
+    small_wait(5)
     tiles = [[jnp.zeros((8, 128), F32) for _ in range(4)] for _ in range(3)]
     for i in range(NX):
         new = solved(1, i)
@@ -426,10 +462,18 @@
         bulk_drain(n)
     for it in range(2):
         halo_drain(it)
-        small_drain(it, 0)
-        small_drain(it, 1)
+    for n in range(6):
+        small_drain(n)
     across.wait()
     ms_o[...] = part_o[...] + part_r[...]
+
+
+def hand_over(psi_i, sens_i, psi_o, sens_o, sem):
+    copies = [pltpu.make_async_copy(psi_i, psi_o, sem.at[0]), pltpu.make_async_copy(sens_i, sens_o, sem.at[1])]
+    for copy in copies:
+        copy.start()
+    for copy in copies:
+        copy.wait()
 
 
 def on_device(
@@ -447,7 +491,7 @@
     psi, sens = pl.pallas_call(
         kernel,
         name="adjoint",
-        out_shape=(jax.ShapeDtypeStruct(cell, F32), jax.ShapeDtypeStruct((3, 8, 512), F32)),
+        out_shape=(pltpu.VMEM(cell, F32), pltpu.VMEM((3, 8, 512), F32)),
         in_specs=[far] * 11 + [scalars] * 2,
         out_specs=(near, near),
         scratch_shapes=[
@@ -460,8 +504,8 @@
             vm(2, 6, 12, 8, 128), vm(2, 6, 12, 8, 128), vm(6, 12, 8, 128),
             vm(*matrix), vm(*matrix), vm(*matrix), vm(*matrix), vm(*matrix), vm(*matrix), vm(*matrix), vm(*matrix),
             vm(3, 8, 512), vm(3, 8, 512),
-            dma((11,)), dma((3, 8)), dma((3, 8)), dma((4, 8)), dma((4, 8)), dma((2, 4)), dma((2, 4)),
-            dma((7,)), dma((2,)),
+            dma((11,)), dma((7, 8)), dma((7, 8)), dma((6, 8)), dma((6, 8)), dma((2, 4)), dma((2, 4)),
+            dma((9,)), dma((2,)),
         ],
         compiler_params=pltpu.CompilerParams(
             collective_id=0, has_side_effects=True, vmem_limit_bytes=58 * 2**20),
@@ -471,6 +515,14 @@
         pack(near_lower), pack(far_lower), pack(y_inverse), z_inverse, pack(sens_terms),
         wall_mask, cond_index, weight_table,
     )
+    psi, sens = pl.pallas_call(
+        hand_over,
+        name="hand_over",
+        out_shape=(jax.ShapeDtypeStruct(cell, F32), jax.ShapeDtypeStruct((3, 8, 512), F32)),
+        in_specs=[far, far],
+        out_specs=(far, far),
+        scratch_shapes=[dma((2,))],
+    )(pltpu.with_memory_space_constraint(psi, pltpu.VMEM), pltpu.with_memory_space_constraint(sens, pltpu.VMEM))
     return unpack(psi), jnp.transpose(sens, (1, 0, 2))
 
 

time: 84.6 us -> 71.8 us (0.85)
  Pallas kernels: 80.7 us -> 70.8 us
  local copies, waits for them, and re-layouts: 3.04 us -> 0 us
    pallas_call x1 -> x2, Pallas kernels: 80.7 us -> 70.8 us  [the longest x1 70.1 us: on_device(): pl.pallas_call(kernel, name='adjoint', out_shape=(pltpu.VMEM(cell, F32),...]
    unnamed x2 -> x0, local copies, waits for them, and re-layouts: 3.04 us -> none
where the time goes in v2:
time: 71.8 us; the launch traced here: 71.5 us
  Pallas kernels  70.8 us (99%)
    pallas_call x1, Pallas kernels, on_device(): pl.pallas_call(kernel, name='adjoint', out_shape=(pltpu.VMEM(cell, F32),...  70.1 us

profile of v2, /device:TPU:8, one launch (start us, length us, event | category | flops | bytes accessed | tf_op | source)
XLA Modules:
  0.0 71.5 jit_solution(2410948255023398918)
XLA Ops:
  0.6 70.1 %adjoint.1 = (f32[8,6,8,128]{3,2,1,0:T(8,128)S(1)}, f32[3,8,512]{2,1,0:T(8,128)S(1)}) custom-call(f32[8,6,8,128]{3,2,1,0:T(8,128)} %bitcast.78, f32[8,6,8,128]{3,2,1,0:T(8,128)} %bitcast.79, f32[8,6,6,8,128]{4,3,2,1,0:T(8,128)} %bitcast.71, f32[8,6,6,8,128]{4,3,2,1,0:T(8,128)} %bitcast.72, f32[8,6,6,8,128]{4,3,2,1,0:T(8,128)} %bitcast.73, ...), custom_call_target="tpu_custom_call" | custom-call | flops 100000000 | bytes 9000000 | tf_op jit(solution)/shard_map/adjoint/pallas_call | solution.py:491
  70.8 0.7 hand_over.1

commit v3 on v2

--- a/solution.py
+++ b/solution.py
@@ -124,7 +124,7 @@
     bulk = (
         (resp.reshape(720, 8, 128).at[576:720], m_r, lambda x: (x > 0) & (x < NX - 1), 1, (0, 144), 0),
         (st_n.reshape(144, 8, 128), n_r, lambda x: (x > 0) & (x < NX - 1), -1, (0, 48, 96, 144), 1),
-        (st_q.reshape(144, 8, 128), q_r, lambda x: x > 0, -1, (0, 48, 108, 144), 4),
+        (st_q.reshape(144, 8, 128), q_r, lambda x: x > 0, -1, (0, 32, 96, 144), 4),
     )
 
     def bulk_copy(n, d, source, part):

time: 71.8 us -> 71.7 us (level)
  no operation moved by 1% of the time
where the time goes in v3:
time: 71.7 us; the launch traced here: 71.6 us
  Pallas kernels  70.9 us (99%)
    pallas_call x1, Pallas kernels, on_device(): pl.pallas_call(kernel, name='adjoint', out_shape=(pltpu.VMEM(cell, F32),...  70.2 us

profile of v3, /device:TPU:8, one launch (start us, length us, event | category | flops | bytes accessed | tf_op | source)
XLA Modules:
  0.0 71.6 jit_solution(18076890127724594986)
XLA Ops:
  0.6 70.2 %adjoint.1 = (f32[8,6,8,128]{3,2,1,0:T(8,128)S(1)}, f32[3,8,512]{2,1,0:T(8,128)S(1)}) custom-call(f32[8,6,8,128]{3,2,1,0:T(8,128)} %bitcast.78, f32[8,6,8,128]{3,2,1,0:T(8,128)} %bitcast.79, f32[8,6,6,8,128]{4,3,2,1,0:T(8,128)} %bitcast.71, f32[8,6,6,8,128]{4,3,2,1,0:T(8,128)} %bitcast.72, f32[8,6,6,8,128]{4,3,2,1,0:T(8,128)} %bitcast.73, ...), custom_call_target="tpu_custom_call" | custom-call | flops 100000000 | bytes 9000000 | tf_op jit(solution)/shard_map/adjoint/pallas_call | solution.py:491
  70.9 0.7 hand_over.1
